TPU v7x, 256 devices: a whole 4x4x8 slice. The times are simulated.
256 devices in a mesh: seq: 32 (over z, y), ch: 8 (over x, core).
Axes of the slice: x: 4, y: 4, z: 8, core: 2. Of those that a mesh axis runs over, the one named last changes fastest.
Arguments:
- tokens: bfloat16 [8192, 4096], P('seq'), may hold values from -6 to 6
- in_weight: bfloat16 [4096, 3, 2048], P(None, None, 'ch'), may hold values from -0.09375 to 0.09375
- filter_taps: float32 [8192, 2048], P('seq', 'ch'), may hold values from -120 to 120
- skip_gain: float32 [2048], P('ch'), may hold values from -1 to 1
- out_weight: bfloat16 [2048, 4096], P(None, 'ch'), may hold values from -0.125 to 0.125
- grad_out: bfloat16 [8192, 4096], P('seq', 'ch'), may hold values from -6 to 6
Outputs:
- output: bfloat16 [8192, 4096], P('seq', 'ch')
- grad_tokens: bfloat16 [8192, 4096], P('seq', 'ch')
- grad_taps: float32 [8192, 2048], P('seq', 'ch')
All inputs are finite; a program needn't handle non-finite values.
Results may differ from a plain program's by a relative error of at most 0.019.
Values may be sent and summed in bfloat16 or wider, within the bound.
A program may use at most 128 MiB of HBM per device.

v0:
```python
import functools
import math

import jax
import jax.numpy as jnp
import ml_dtypes
import numpy as np
from jax import lax
from jax.experimental import pallas as pl
from jax.experimental.pallas import tpu as pltpu
from jax.sharding import PartitionSpec as P

MESH = pl.DeviceIdType.MESH
F32 = jnp.float32
BF16 = jnp.bfloat16
LANES = 128


def tables(ranks, per):
    rows = 2 * ranks
    length = rows * LANES
    first = np.arange(rows)
    low = first + 0.25
    angle = 2.0 * np.pi * np.outer(low, first) / rows
    eye = np.eye(per)
    cross = np.concatenate(
        [np.kron(np.cos(angle), eye), np.kron(-np.sin(angle), eye)], axis=0
    )
    cross_back = cross.T / length
    turn = 2.0 * np.pi * np.outer(np.repeat(low, per), np.arange(LANES)) / length
    inner = 2.0 * np.pi * np.outer(np.arange(LANES), np.arange(LANES)) / LANES
    cosine, sine = np.cos(inner), np.sin(inner)
    local = np.block([[cosine, -sine], [sine, cosine]])
    narrow = ml_dtypes.bfloat16
    return (
        cross.astype(narrow),
        cross_back.astype(narrow),
        local.astype(narrow),
        local.T.astype(narrow),
        np.cos(turn).astype(np.float32),
        (-np.sin(turn)).astype(np.float32),
    )


def dot(left, right):
    return jnp.dot(left, right, preferred_element_type=F32)


def dot_nt(left, right):
    return lax.dot_general(
        left, right, (((1,), (1,)), ((), ())), preferred_element_type=F32
    )


def kernel(
    ranks,
    chans,
    *refs,
):
    (
        tok_h, win_h, taps_h, skip_ref, wout_h, gout_h,
        cross_h, back_h, local_h, unlocal_h, tr_h, ti_h,
        out_h, gtok_h, gtaps_h,
        tok, win, taps, wout, gout, cross, back, local, unlocal, tr, ti,
        mixed, pre, gg, gc, spec_t, spec_p,
        s_taps, s_pre, s_grad, s_conv, s_gpre, s_gtaps,
        r_taps, r_pre, r_grad, r_conv, r_gpre, r_gtaps,
        a_send, a_got, a_own, a_sum, a_part,
        gath, gm,
        b_send, b_got, b_own, b_sum, b_part,
        o_out, o_gtok, o_gtaps,
        load_sem, store_sem, seq_send, seq_recv,
        pair_send, a_sem, b_sem, x_send, a_x_sem, b_x_sem,
        ag_send, ag_sem,
    ) = refs
    seq = lax.axis_index("seq")
    ch = lax.axis_index("ch")
    chips = chans // 2
    x, core = ch // 2, ch % 2
    partner = (seq, ch + 1 - 2 * core)
    block, width = tok.shape
    local_ch = win.shape[2]
    per = local_ch // ranks
    feats = gout.shape[1]
    half = ranks * 2 * per
    scale = (ranks * block) ** -0.5

    def peer(step):
        return (x + step) % chips

    order = [k for k in (2, 1, 3) if k < chips]

    loads = [
        (gout_h, gout), (wout_h, wout), (taps_h, taps), (tok_h, tok),
        (win_h.at[0], win.at[0]), (win_h.at[1], win.at[1]), (win_h.at[2], win.at[2]),
        (cross_h, cross), (local_h, local), (tr_h, tr), (ti_h, ti),
        (unlocal_h, unlocal), (back_h, back),
    ]
    copies = [
        pltpu.make_async_copy(src, dst, load_sem.at[i])
        for i, (src, dst) in enumerate(loads)
    ]
    for copy in copies:
        copy.start()

    barrier = pltpu.get_barrier_semaphore()

    def greet(k, carry):
        pl.semaphore_signal(
            barrier, inc=1, device_id=((seq + k) % ranks, ch), device_id_type=MESH
        )
        return carry

    lax.fori_loop(1, ranks, greet, 0)
    pl.semaphore_signal(barrier, inc=1, device_id=partner, device_id_type=MESH)
    for k in order:
        pl.semaphore_signal(
            barrier, inc=1, device_id=(seq, 2 * peer(k) + core), device_id_type=MESH
        )

    def remote(src, dst, send, recv, device):
        copy = pltpu.make_async_remote_copy(
            src_ref=src, dst_ref=dst, send_sem=send, recv_sem=recv,
            device_id=device, device_id_type=MESH,
        )
        copy.start()

    def wait(ref, sem):
        pltpu.make_async_copy(ref, ref, sem).wait()

    def spread(buf, got, n):
        def send(k, carry):
            to = (seq + k) % ranks
            remote(buf.at[to], got.at[seq], seq_send.at[n], seq_recv.at[n], (to, ch))
            return carry

        lax.fori_loop(1, ranks, send, 0)
        got[seq] = buf[seq]

    def arrive(got, n):
        wait(got.at[pl.ds(0, ranks - 1)], seq_recv.at[n])

    def to_pieces(value, buf):
        turned = value.T
        parts = [
            turned[:, i * LANES : (i + 1) * LANES].reshape(ranks, per, LANES)
            for i in range(2)
        ]
        buf[...] = jnp.concatenate(parts, axis=1).astype(BF16)

    def from_pieces(got):
        parts = got[...].astype(F32)
        turned = jnp.concatenate(
            [
                parts[:, i * per : (i + 1) * per, :].reshape(local_ch, LANES)
                for i in range(2)
            ],
            axis=1,
        )
        return turned.T

    def spectrum(got):
        flat = got[...].reshape(half, LANES)
        both = dot(cross[...], flat)
        re, im = both[:half], both[half:]
        cosine, sine = tr[...], ti[...]
        turned = jnp.concatenate(
            [re * cosine - im * sine, re * sine + im * cosine], axis=1
        )
        return dot(turned.astype(BF16), local[...])

    def inverse(re, im, buf):
        both = dot(jnp.concatenate([re, im], axis=1).astype(BF16), unlocal[...])
        re, im = both[:, :LANES], both[:, LANES:]
        cosine, sine = tr[...], ti[...]
        turned = jnp.concatenate(
            [re * cosine + im * sine, im * cosine - re * sine], axis=0
        )
        result = dot(back[...], turned.astype(BF16))
        buf[...] = result.astype(BF16).reshape(ranks, 2 * per, LANES)

    copies[0].wait()
    copies[1].wait()

    def feature_chunk(index):
        rows = wout[pl.ds(pl.multiple_of(index * local_ch, local_ch), local_ch), :]
        return dot_nt(gout[...], rows)

    for i, k in enumerate(order + [0]):
        to = peer(k)
        a_send[to] = feature_chunk(2 * to + 1 - core).astype(BF16)
        if i == 0:
            pl.semaphore_wait(barrier, ranks - 1 + 1 + len(order))
        remote(a_send.at[to], a_got.at[to], pair_send.at[0], a_sem.at[to], partner)
    for k in order + [0]:
        to = peer(k)
        a_own[to] = feature_chunk(2 * to + core)

    copies[2].wait()
    to_pieces(taps[...] * scale, s_taps)

    for k in order:
        to = peer(k)
        wait(a_got.at[to], a_sem.at[to])
        a_sum[to] = (a_own[to] + a_got[to].astype(F32)).astype(BF16)
        remote(
            a_sum.at[to], a_part.at[x], x_send.at[0], a_x_sem.at[x], (seq, 2 * to + core)
        )

    spread(s_taps, r_taps, 0)

    for i in (3, 4, 5, 6):
        copies[i].wait()

    def project(i, carry):
        mixed[i] = dot(tok[...], win[i]).astype(BF16)
        return carry

    lax.fori_loop(0, 3, project, 0)
    pre[...] = mixed[1].astype(F32) * mixed[0].astype(F32)
    to_pieces(pre[...], s_pre)
    spread(s_pre, r_pre, 1)

    wait(a_got.at[x], a_sem.at[x])
    gg[...] = a_own[x] + a_got[x].astype(F32)
    for k in (1, 3, 2):
        if k < chips:
            wait(a_part.at[peer(k)], a_x_sem.at[peer(k)])
            gg[...] += a_part[peer(k)].astype(F32)
    gc[...] = gg[...] * mixed[2].astype(F32)
    to_pieces(gc[...], s_grad)
    spread(s_grad, r_grad, 2)

    for i in range(7, 13):
        copies[i].wait()
    arrive(r_taps, 0)
    spec_t[...] = spectrum(r_taps)
    arrive(r_pre, 1)
    spec_p[...] = spectrum(r_pre)
    t_re, t_im = spec_t[:, :LANES], spec_t[:, LANES:]
    p_re, p_im = spec_p[:, :LANES], spec_p[:, LANES:]
    inverse(t_re * p_re - t_im * p_im, t_re * p_im + t_im * p_re, s_conv)
    spread(s_conv, r_conv, 3)
    arrive(r_grad, 2)
    spec_g = spectrum(r_grad)
    g_re, g_im = spec_g[:, :LANES], spec_g[:, LANES:]
    t_re, t_im = spec_t[:, :LANES], spec_t[:, LANES:]
    inverse(t_re * g_re + t_im * g_im, t_re * g_im - t_im * g_re, s_gpre)
    spread(s_gpre, r_gpre, 4)
    p_re, p_im = spec_p[:, :LANES], spec_p[:, LANES:]
    inverse(p_re * g_re + p_im * g_im, p_re * g_im - p_im * g_re, s_gtaps)
    spread(s_gtaps, r_gtaps, 5)

    arrive(r_conv, 3)
    conv = from_pieces(r_conv) + skip_ref[...] * pre[...]
    gath[ch] = (mixed[2].astype(F32) * conv).astype(BF16)
    for k in order:
        remote(
            gath.at[ch], gath.at[ch], ag_send, ag_sem.at[ch], (seq, 2 * peer(k) + core)
        )
    remote(gath.at[ch], gath.at[ch], ag_send, ag_sem.at[ch], partner)
    gm[2] = (gg[...] * conv).astype(BF16)

    arrive(r_gpre, 4)
    grad_pre = from_pieces(r_gpre) + skip_ref[...] * gc[...]
    gm[0] = (grad_pre * mixed[1].astype(F32)).astype(BF16)
    gm[1] = (grad_pre * mixed[0].astype(F32)).astype(BF16)

    def input_chunk(index):
        rows = pl.ds(pl.multiple_of(index * feats, feats), feats)
        total = dot_nt(gm[0], win[0, rows, :])
        total += dot_nt(gm[1], win[1, rows, :])
        return total + dot_nt(gm[2], win[2, rows, :])

    for k in order + [0]:
        to = peer(k)
        b_send[to] = input_chunk(2 * to + 1 - core).astype(BF16)
        remote(b_send.at[to], b_got.at[to], pair_send.at[1], b_sem.at[to], partner)
    for k in order:
        to = peer(k)
        b_own[to] = input_chunk(2 * to + core)
        wait(b_got.at[to], b_sem.at[to])
        b_sum[to] = (b_own[to] + b_got[to].astype(F32)).astype(BF16)
        remote(
            b_sum.at[to], b_part.at[x], x_send.at[1], b_x_sem.at[x], (seq, 2 * to + core)
        )
    for k in (1, 3, 2):
        if k < chips:
            slot = 2 * peer(k) + core
            wait(gath.at[slot], ag_sem.at[slot])
            remote(gath.at[slot], gath.at[slot], ag_send, ag_sem.at[slot], partner)
    b_own[x] = input_chunk(2 * x + core)

    for k in range(chips):
        slot = 2 * peer(k) + 1 - core
        wait(gath.at[slot], ag_sem.at[slot])

    def output_rows(index):
        rows = wout[pl.ds(pl.multiple_of(index * local_ch, local_ch), local_ch), :]
        return dot(gath[index], rows)

    total = output_rows(0)
    for i in range(1, chans):
        total += output_rows(i)
    o_out[...] = total.astype(BF16)
    out_copy = pltpu.make_async_copy(o_out, out_h, store_sem.at[0])
    out_copy.start()

    arrive(r_gtaps, 5)
    o_gtaps[...] = from_pieces(r_gtaps) * scale
    gtaps_copy = pltpu.make_async_copy(o_gtaps, gtaps_h, store_sem.at[1])
    gtaps_copy.start()

    wait(b_got.at[x], b_sem.at[x])
    b_own[x] += b_got[x].astype(F32)
    for k in (1, 3, 2):
        if k < chips:
            wait(b_part.at[peer(k)], b_x_sem.at[peer(k)])
            b_own[x] += b_part[peer(k)].astype(F32)
    o_gtok[...] = b_own[x].astype(BF16)
    gtok_copy = pltpu.make_async_copy(o_gtok, gtok_h, store_sem.at[2])
    gtok_copy.start()

    for n, buf in enumerate((s_taps, s_pre, s_grad, s_conv, s_gpre, s_gtaps)):
        wait(buf.at[pl.ds(0, ranks - 1)], seq_send.at[n])
    wait(a_send, pair_send.at[0])
    wait(b_send, pair_send.at[1])
    if order:
        wait(a_sum.at[pl.ds(0, len(order))], x_send.at[0])
        wait(b_sum.at[pl.ds(0, len(order))], x_send.at[1])
    wait(gath.at[pl.ds(0, 2 * len(order) + 1)], ag_send)
    out_copy.wait()
    gtaps_copy.wait()
    gtok_copy.wait()


def on_device(ranks, chans, tokens, in_weight, filter_taps, skip_gain, out_weight, grad_out):
    block, width = tokens.shape
    local_ch = in_weight.shape[2]
    feats = grad_out.shape[1]
    per = local_ch // ranks
    chips = chans // 2
    half = 2 * ranks * per
    weight = jnp.transpose(in_weight, (1, 0, 2))
    constants = tables(ranks, per)
    hbm = pl.BlockSpec(memory_space=pl.ANY)
    vmem = pl.BlockSpec(memory_space=pltpu.VMEM)
    piece = (ranks, 2 * per, LANES)
    chunk = (chips, block, local_ch)
    wide = (chips, block, feats)
    scratch = [
        pltpu.VMEM(tokens.shape, BF16),
        pltpu.VMEM(weight.shape, BF16),
        pltpu.VMEM(filter_taps.shape, F32),
        pltpu.VMEM(out_weight.shape, BF16),
        pltpu.VMEM(grad_out.shape, BF16),
        pltpu.VMEM((2 * half, half), BF16),
        pltpu.VMEM((half, 2 * half), BF16),
        pltpu.VMEM((2 * LANES, 2 * LANES), BF16),
        pltpu.VMEM((2 * LANES, 2 * LANES), BF16),
        pltpu.VMEM((half, LANES), F32),
        pltpu.VMEM((half, LANES), F32),
        pltpu.VMEM((3, block, local_ch), BF16),
        pltpu.VMEM((block, local_ch), F32),
        pltpu.VMEM((block, local_ch), F32),
        pltpu.VMEM((block, local_ch), F32),
        pltpu.VMEM((half, 2 * LANES), F32),
        pltpu.VMEM((half, 2 * LANES), F32),
        *[pltpu.VMEM(piece, BF16) for _ in range(12)],
        pltpu.VMEM(chunk, BF16),
        pltpu.VMEM(chunk, BF16),
        pltpu.VMEM(chunk, F32),
        pltpu.VMEM(chunk, BF16),
        pltpu.VMEM(chunk, BF16),
        pltpu.VMEM((chans, block, local_ch), BF16),
        pltpu.VMEM((3, block, local_ch), BF16),
        pltpu.VMEM(wide, BF16),
        pltpu.VMEM(wide, BF16),
        pltpu.VMEM(wide, F32),
        pltpu.VMEM(wide, BF16),
        pltpu.VMEM(wide, BF16),
        pltpu.VMEM((block, feats), BF16),
        pltpu.VMEM((block, feats), BF16),
        pltpu.VMEM((block, local_ch), F32),
        pltpu.SemaphoreType.DMA((13,)),
        pltpu.SemaphoreType.DMA((3,)),
        pltpu.SemaphoreType.DMA((6,)),
        pltpu.SemaphoreType.DMA((6,)),
        pltpu.SemaphoreType.DMA((2,)),
        pltpu.SemaphoreType.DMA((chips,)),
        pltpu.SemaphoreType.DMA((chips,)),
        pltpu.SemaphoreType.DMA((2,)),
        pltpu.SemaphoreType.DMA((chips,)),
        pltpu.SemaphoreType.DMA((chips,)),
        pltpu.SemaphoreType.DMA,
        pltpu.SemaphoreType.DMA((chans,)),
    ]
    return pl.pallas_call(
        functools.partial(kernel, ranks, chans),
        out_shape=(
            jax.ShapeDtypeStruct((block, feats), BF16),
            jax.ShapeDtypeStruct((block, feats), BF16),
            jax.ShapeDtypeStruct((block, local_ch), F32),
        ),
        in_specs=[hbm, hbm, hbm, vmem, hbm, hbm] + [hbm] * 6,
        out_specs=(hbm, hbm, hbm),
        scratch_shapes=scratch,
        compiler_params=pltpu.CompilerParams(
            collective_id=0, has_side_effects=True, vmem_limit_bytes=58 * 1024 * 1024
        ),
    )(
        tokens, weight, filter_taps, skip_gain.reshape(1, local_ch), out_weight, grad_out,
        *[jnp.asarray(table) for table in constants],
    )


def solution(mesh):
    placed = (
        P("seq", None),
        P(None, None, "ch"),
        P("seq", "ch"),
        P("ch"),
        P(None, "ch"),
        P("seq", "ch"),
    )
    return jax.shard_map(
        functools.partial(on_device, mesh.shape["seq"], mesh.shape["ch"]),
        mesh=mesh,
        in_specs=placed,
        out_specs=(P("seq", "ch"), P("seq", "ch"), P("seq", "ch")),
        check_vma=False,
    )
```

profile of v0, /device:TPU:1, one launch (start us, length us, event | category | flops | bytes accessed | tf_op | source)
XLA Modules:
  0.0 61.3 jit_solution(8069252209996947280)
XLA Ops:
  0.6 55.7 %shard_map.139 = (bf16[256,512]{1,0:T(8,128)(2,1)}, bf16[256,512]{1,0:T(8,128)(2,1)}, f32[256,256]{1,0:T(8,128)}) custom-call(bf16[256,4096]{1,0:T(8,128)(2,1)} %refs_0_.1, bf16[3,4096,256]{2,1,0:T(8,128)(2,1)} %bitcast.2, f32[256,256]{1,0:T(8,128)} %refs_2_.1, f32[1,256]{1,0:T(1,128)} %bitcast.3, bf16[2048,512]{1,0:T(8,128)(2,1)} %refs_4_.1, ...), custom_call_target="tpu_custom_call" | custom-call | tf_op jit(solution)/shard_map/pallas_call | solution.py:398
  56.3 1.7 %copy.18 = bf16[256,512]{1,0:T(8,128)(2,1)} copy(bf16[256,512]{1,0:T(8,128)(2,1)} %get-tuple-element.6) | data formatting | bytes 524288
  58.0 1.7 %copy.19 = bf16[256,512]{1,0:T(8,128)(2,1)} copy(bf16[256,512]{1,0:T(8,128)(2,1)} %get-tuple-element.7) | data formatting | bytes 524288
  59.7 1.7 %copy.20 = f32[256,256]{1,0:T(8,128)} copy(f32[256,256]{1,0:T(8,128)} %get-tuple-element.8) | data formatting | bytes 524288
where the time goes:
time: 61.5 us; the launch traced here: 61.3 us
  Pallas kernels  55.7 us (91%)
  local copies, waits for them, and re-layouts  5.01 us (8%)
  between operations  0.64 us (1%)
    pallas_call x1, Pallas kernels, on_device(): pl.pallas_call(functools.partial(kernel, ranks, chans), out_shape=(jax.Sh...  55.7 us
    unnamed x3, local copies, waits for them, and re-layouts  5.01 us

commit v1 on v0

--- a/solution.py
+++ b/solution.py
@@ -62,15 +62,15 @@
         cross_h, back_h, local_h, unlocal_h, tr_h, ti_h,
         out_h, gtok_h, gtaps_h,
         tok, win, taps, wout, gout, cross, back, local, unlocal, tr, ti,
-        mixed, pre, gg, gc, spec_t, spec_p,
+        mixed, pre, gg, gc, spec_t, spec_p, spec_g,
         s_taps, s_pre, s_grad, s_conv, s_gpre, s_gtaps,
         r_taps, r_pre, r_grad, r_conv, r_gpre, r_gtaps,
-        a_send, a_got, a_own, a_sum, a_part,
+        a_send, a_got, a_own, a_sum, a_fwd, a_in,
         gath, gm,
-        b_send, b_got, b_own, b_sum, b_part,
+        b_send, b_got, b_own, b_sum, b_fwd, b_in,
         o_out, o_gtok, o_gtaps,
         load_sem, store_sem, seq_send, seq_recv,
-        pair_send, a_sem, b_sem, x_send, a_x_sem, b_x_sem,
+        pair_send, a_sem, b_sem, x_send, a_f_sem, b_f_sem, a_i_sem, b_i_sem,
         ag_send, ag_sem,
     ) = refs
     seq = lax.axis_index("seq")
@@ -84,14 +84,25 @@
     feats = gout.shape[1]
     half = ranks * 2 * per
     scale = (ranks * block) ** -0.5
+    part = block // 2
+    turns = 4 if ranks % 8 == 0 else 1
+    some = ranks // 2
 
     def peer(step):
         return (x + step) % chips
 
-    order = [k for k in (2, 1, 3) if k < chips]
+    def slot_of(rank):
+        z, y = rank // turns, rank % turns
+        return (z % 2) * some + (z // 2) * turns + y
+
+    def rank_of(slot):
+        side, rest = slot // some, slot % some
+        return (2 * (rest // turns) + side) * turns + rest % turns
+
+    mine = slot_of(seq)
 
     loads = [
-        (gout_h, gout), (wout_h, wout), (taps_h, taps), (tok_h, tok),
+        (taps_h, taps), (gout_h, gout), (wout_h, wout), (tok_h, tok),
         (win_h.at[0], win.at[0]), (win_h.at[1], win.at[1]), (win_h.at[2], win.at[2]),
         (cross_h, cross), (local_h, local), (tr_h, tr), (ti_h, ti),
         (unlocal_h, unlocal), (back_h, back),
@@ -100,7 +111,7 @@
         pltpu.make_async_copy(src, dst, load_sem.at[i])
         for i, (src, dst) in enumerate(loads)
     ]
-    for copy in copies:
+    for copy in copies[:3]:
         copy.start()
 
     barrier = pltpu.get_barrier_semaphore()
@@ -113,7 +124,7 @@
 
     lax.fori_loop(1, ranks, greet, 0)
     pl.semaphore_signal(barrier, inc=1, device_id=partner, device_id_type=MESH)
-    for k in order:
+    for k in (1, 2, 3):
         pl.semaphore_signal(
             barrier, inc=1, device_id=(seq, 2 * peer(k) + core), device_id_type=MESH
         )
@@ -131,22 +142,49 @@
     def spread(buf, got, n):
         def send(k, carry):
             to = (seq + k) % ranks
-            remote(buf.at[to], got.at[seq], seq_send.at[n], seq_recv.at[n], (to, ch))
+            remote(
+                buf.at[slot_of(to)], got.at[seq], seq_send.at[n], seq_recv.at[n], (to, ch)
+            )
             return carry
 
         lax.fori_loop(1, ranks, send, 0)
-        got[seq] = buf[seq]
+        got[seq] = buf[mine]
+
+    def spread_side(buf, got, n, side):
+        def send(k, carry):
+            slot = side * some + (mine + k) % some
+            to = rank_of(slot)
+
+            @pl.when(to != seq)
+            def _():
+                remote(
+                    buf.at[slot], got.at[seq], seq_send.at[n], seq_recv.at[n], (to, ch)
+                )
+
+            return carry
+
+        lax.fori_loop(0, some, send, 0)
+
+    def give_back(buf, got, n):
+        def send(k, carry):
+            to = (seq + k) % ranks
+            remote(buf.at[to], got.at[mine], seq_send.at[n], seq_recv.at[n], (to, ch))
+            return carry
+
+        lax.fori_loop(1, ranks, send, 0)
+        got[mine] = buf[seq]
 
     def arrive(got, n):
         wait(got.at[pl.ds(0, ranks - 1)], seq_recv.at[n])
 
-    def to_pieces(value, buf):
+    def to_pieces(value, buf, first):
         turned = value.T
+        count = turned.shape[0] // per
         parts = [
-            turned[:, i * LANES : (i + 1) * LANES].reshape(ranks, per, LANES)
+            turned[:, i * LANES : (i + 1) * LANES].reshape(count, per, LANES)
             for i in range(2)
         ]
-        buf[...] = jnp.concatenate(parts, axis=1).astype(BF16)
+        buf[first : first + count] = jnp.concatenate(parts, axis=1).astype(BF16)
 
     def from_pieces(got):
         parts = got[...].astype(F32)
@@ -179,60 +217,114 @@
         result = dot(back[...], turned.astype(BF16))
         buf[...] = result.astype(BF16).reshape(ranks, 2 * per, LANES)
 
+    near = (1, 3)
+
+    def rows(d):
+        return pl.ds(d * part, part)
+
+    def columns(ref, h):
+        count = ref.shape[-1] // 2
+        return slice(h * count, (h + 1) * count)
+
+    def fold(own, got, sem, k):
+        to = peer(k)
+        wait(got.at[to], sem.at[to])
+        own[to] = own[to] + got[to].astype(F32)
+
+    def far(own, sums, fwd, f_sem, n, h):
+        sums[0, h] = own[peer(2), :, columns(own, h)].astype(BF16)
+        for d in (0, 1):
+            remote(
+                sums.at[0, h, rows(d)], fwd.at[d, h], x_send.at[n], f_sem.at[d, h],
+                (seq, 2 * peer(near[d]) + core),
+            )
+
+    def plain(own, sums, into, i_sem, n, h):
+        for d in (0, 1):
+            to = peer(near[d])
+            sums[1 + d, h, rows(1 - d)] = own[
+                to, rows(1 - d), columns(own, h)
+            ].astype(BF16)
+            remote(
+                sums.at[1 + d, h, rows(1 - d)], into.at[d, h, rows(1 - d)],
+                x_send.at[n], i_sem.at[0, d, h], (seq, 2 * to + core),
+            )
+
+    def onward(own, sums, fwd, f_sem, into, i_sem, n, h):
+        for d in (0, 1):
+            to = peer(near[d])
+            wait(fwd.at[d, h], f_sem.at[d, h])
+            sums[1 + d, h, rows(d)] = (
+                own[to, rows(d), columns(own, h)] + fwd[d, h].astype(F32)
+            ).astype(BF16)
+            remote(
+                sums.at[1 + d, h, rows(d)], into.at[d, h, rows(d)],
+                x_send.at[n], i_sem.at[1, d, h], (seq, 2 * to + core),
+            )
+
+    def collect(own, into, i_sem, h):
+        for d in (0, 1):
+            wait(into.at[d, h, rows(1 - d)], i_sem.at[0, d, h])
+            wait(into.at[d, h, rows(d)], i_sem.at[1, d, h])
+        return own[x, :, columns(own, h)] + (
+            into[0, h].astype(F32) + into[1, h].astype(F32)
+        )
+
     copies[0].wait()
+    to_pieces(taps[...] * scale, s_taps, 0)
+    pl.semaphore_wait(barrier, ranks - 1 + 1 + 3)
+    spread(s_taps, r_taps, 0)
+
     copies[1].wait()
+    copies[2].wait()
+    for copy in copies[3:7]:
+        copy.start()
 
     def feature_chunk(index):
-        rows = wout[pl.ds(pl.multiple_of(index * local_ch, local_ch), local_ch), :]
-        return dot_nt(gout[...], rows)
-
-    for i, k in enumerate(order + [0]):
+        weights = wout[pl.ds(pl.multiple_of(index * local_ch, local_ch), local_ch), :]
+        return dot_nt(gout[...], weights)
+
+    for k in (2, 1, 3, 0):
         to = peer(k)
         a_send[to] = feature_chunk(2 * to + 1 - core).astype(BF16)
-        if i == 0:
-            pl.semaphore_wait(barrier, ranks - 1 + 1 + len(order))
         remote(a_send.at[to], a_got.at[to], pair_send.at[0], a_sem.at[to], partner)
-    for k in order + [0]:
+    for k in (2, 1, 3, 0):
         to = peer(k)
         a_own[to] = feature_chunk(2 * to + core)
-
-    copies[2].wait()
-    to_pieces(taps[...] * scale, s_taps)
-
-    for k in order:
-        to = peer(k)
-        wait(a_got.at[to], a_sem.at[to])
-        a_sum[to] = (a_own[to] + a_got[to].astype(F32)).astype(BF16)
-        remote(
-            a_sum.at[to], a_part.at[x], x_send.at[0], a_x_sem.at[x], (seq, 2 * to + core)
-        )
-
-    spread(s_taps, r_taps, 0)
-
-    for i in (3, 4, 5, 6):
-        copies[i].wait()
-
-    def project(i, carry):
-        mixed[i] = dot(tok[...], win[i]).astype(BF16)
-        return carry
-
-    lax.fori_loop(0, 3, project, 0)
+    fold(a_own, a_got, a_sem, 2)
+    far(a_own, a_sum, a_fwd, a_f_sem, 0, 0)
+    fold(a_own, a_got, a_sem, 1)
+    fold(a_own, a_got, a_sem, 3)
+    plain(a_own, a_sum, a_in, a_i_sem, 0, 0)
+    far(a_own, a_sum, a_fwd, a_f_sem, 0, 1)
+    fold(a_own, a_got, a_sem, 0)
+
+    copies[3].wait()
+    copies[4].wait()
+    mixed[0] = dot(tok[...], win[0]).astype(BF16)
+    onward(a_own, a_sum, a_fwd, a_f_sem, a_in, a_i_sem, 0, 0)
+    plain(a_own, a_sum, a_in, a_i_sem, 0, 1)
+    copies[5].wait()
+    copies[6].wait()
+    for copy in copies[7:]:
+        copy.start()
+    mixed[1] = dot(tok[...], win[1]).astype(BF16)
+    onward(a_own, a_sum, a_fwd, a_f_sem, a_in, a_i_sem, 0, 1)
     pre[...] = mixed[1].astype(F32) * mixed[0].astype(F32)
-    to_pieces(pre[...], s_pre)
+    to_pieces(pre[...], s_pre, 0)
     spread(s_pre, r_pre, 1)
-
-    wait(a_got.at[x], a_sem.at[x])
-    gg[...] = a_own[x] + a_got[x].astype(F32)
-    for k in (1, 3, 2):
-        if k < chips:
-            wait(a_part.at[peer(k)], a_x_sem.at[peer(k)])
-            gg[...] += a_part[peer(k)].astype(F32)
-    gc[...] = gg[...] * mixed[2].astype(F32)
-    to_pieces(gc[...], s_grad)
-    spread(s_grad, r_grad, 2)
-
-    for i in range(7, 13):
-        copies[i].wait()
+    mixed[2] = dot(tok[...], win[2]).astype(BF16)
+
+    for h in (0, 1):
+        cut = columns(gg, h)
+        gg[:, cut] = collect(a_own, a_in, a_i_sem, h)
+        gc[:, cut] = gg[:, cut] * mixed[2, :, cut].astype(F32)
+        to_pieces(gc[:, cut], s_grad, h * some)
+        spread_side(s_grad, r_grad, 2, h)
+    r_grad[seq] = s_grad[mine]
+
+    for copy in copies[7:]:
+        copy.wait()
     arrive(r_taps, 0)
     spec_t[...] = spectrum(r_taps)
     arrive(r_pre, 1)
@@ -240,21 +332,21 @@
     t_re, t_im = spec_t[:, :LANES], spec_t[:, LANES:]
     p_re, p_im = spec_p[:, :LANES], spec_p[:, LANES:]
     inverse(t_re * p_re - t_im * p_im, t_re * p_im + t_im * p_re, s_conv)
-    spread(s_conv, r_conv, 3)
+    give_back(s_conv, r_conv, 3)
     arrive(r_grad, 2)
-    spec_g = spectrum(r_grad)
+    spec_g[...] = spectrum(r_grad)
     g_re, g_im = spec_g[:, :LANES], spec_g[:, LANES:]
     t_re, t_im = spec_t[:, :LANES], spec_t[:, LANES:]
     inverse(t_re * g_re + t_im * g_im, t_re * g_im - t_im * g_re, s_gpre)
-    spread(s_gpre, r_gpre, 4)
+    give_back(s_gpre, r_gpre, 4)
     p_re, p_im = spec_p[:, :LANES], spec_p[:, LANES:]
+    g_re, g_im = spec_g[:, :LANES], spec_g[:, LANES:]
     inverse(p_re * g_re + p_im * g_im, p_re * g_im - p_im * g_re, s_gtaps)
-    spread(s_gtaps, r_gtaps, 5)
 
     arrive(r_conv, 3)
     conv = from_pieces(r_conv) + skip_ref[...] * pre[...]
     gath[ch] = (mixed[2].astype(F32) * conv).astype(BF16)
-    for k in order:
+    for k in (2, 1, 3):
         remote(
             gath.at[ch], gath.at[ch], ag_send, ag_sem.at[ch], (seq, 2 * peer(k) + core)
         )
@@ -267,37 +359,41 @@
     gm[1] = (grad_pre * mixed[0].astype(F32)).astype(BF16)
 
     def input_chunk(index):
-        rows = pl.ds(pl.multiple_of(index * feats, feats), feats)
-        total = dot_nt(gm[0], win[0, rows, :])
-        total += dot_nt(gm[1], win[1, rows, :])
-        return total + dot_nt(gm[2], win[2, rows, :])
-
-    for k in order + [0]:
+        span = pl.ds(pl.multiple_of(index * feats, feats), feats)
+        total = dot_nt(gm[0], win[0, span, :])
+        total += dot_nt(gm[1], win[1, span, :])
+        return total + dot_nt(gm[2], win[2, span, :])
+
+    for k in (2, 1, 3, 0):
         to = peer(k)
         b_send[to] = input_chunk(2 * to + 1 - core).astype(BF16)
         remote(b_send.at[to], b_got.at[to], pair_send.at[1], b_sem.at[to], partner)
-    for k in order:
-        to = peer(k)
-        b_own[to] = input_chunk(2 * to + core)
-        wait(b_got.at[to], b_sem.at[to])
-        b_sum[to] = (b_own[to] + b_got[to].astype(F32)).astype(BF16)
-        remote(
-            b_sum.at[to], b_part.at[x], x_send.at[1], b_x_sem.at[x], (seq, 2 * to + core)
-        )
+    b_own[peer(2)] = input_chunk(2 * peer(2) + core)
+    fold(b_own, b_got, b_sem, 2)
+    for h in (0, 1):
+        far(b_own, b_sum, b_fwd, b_f_sem, 1, h)
+    for k in (1, 3):
+        b_own[peer(k)] = input_chunk(2 * peer(k) + core)
+        fold(b_own, b_got, b_sem, k)
+    for h in (0, 1):
+        plain(b_own, b_sum, b_in, b_i_sem, 1, h)
+    give_back(s_gtaps, r_gtaps, 5)
+    b_own[x] = input_chunk(2 * x + core)
+    fold(b_own, b_got, b_sem, 0)
+    for h in (0, 1):
+        onward(b_own, b_sum, b_fwd, b_f_sem, b_in, b_i_sem, 1, h)
+
     for k in (1, 3, 2):
-        if k < chips:
-            slot = 2 * peer(k) + core
-            wait(gath.at[slot], ag_sem.at[slot])
-            remote(gath.at[slot], gath.at[slot], ag_send, ag_sem.at[slot], partner)
-    b_own[x] = input_chunk(2 * x + core)
-
+        slot = 2 * peer(k) + core
+        wait(gath.at[slot], ag_sem.at[slot])
+        remote(gath.at[slot], gath.at[slot], ag_send, ag_sem.at[slot], partner)
     for k in range(chips):
         slot = 2 * peer(k) + 1 - core
         wait(gath.at[slot], ag_sem.at[slot])
 
     def output_rows(index):
-        rows = wout[pl.ds(pl.multiple_of(index * local_ch, local_ch), local_ch), :]
-        return dot(gath[index], rows)
+        weights = wout[pl.ds(pl.multiple_of(index * local_ch, local_ch), local_ch), :]
+        return dot(gath[index], weights)
 
     total = output_rows(0)
     for i in range(1, chans):
@@ -311,13 +407,8 @@
     gtaps_copy = pltpu.make_async_copy(o_gtaps, gtaps_h, store_sem.at[1])
     gtaps_copy.start()
 
-    wait(b_got.at[x], b_sem.at[x])
-    b_own[x] += b_got[x].astype(F32)
-    for k in (1, 3, 2):
-        if k < chips:
-            wait(b_part.at[peer(k)], b_x_sem.at[peer(k)])
-            b_own[x] += b_part[peer(k)].astype(F32)
-    o_gtok[...] = b_own[x].astype(BF16)
+    for h in (0, 1):
+        o_gtok[:, columns(o_gtok, h)] = collect(b_own, b_in, b_i_sem, h).astype(BF16)
     gtok_copy = pltpu.make_async_copy(o_gtok, gtok_h, store_sem.at[2])
     gtok_copy.start()
 
@@ -325,13 +416,23 @@
         wait(buf.at[pl.ds(0, ranks - 1)], seq_send.at[n])
     wait(a_send, pair_send.at[0])
     wait(b_send, pair_send.at[1])
-    if order:
-        wait(a_sum.at[pl.ds(0, len(order))], x_send.at[0])
-        wait(b_sum.at[pl.ds(0, len(order))], x_send.at[1])
-    wait(gath.at[pl.ds(0, 2 * len(order) + 1)], ag_send)
+    wait(a_sum, x_send.at[0])
+    wait(b_sum, x_send.at[1])
+    wait(gath.at[pl.ds(0, 7)], ag_send)
     out_copy.wait()
     gtaps_copy.wait()
     gtok_copy.wait()
+
+
+def place(a, b, c, d, e, f, sem):
+    copies = [
+        pltpu.make_async_copy(src, dst, sem.at[i])
+        for i, (src, dst) in enumerate(((a, d), (b, e), (c, f)))
+    ]
+    for copy in copies:
+        copy.start()
+    for copy in copies:
+        copy.wait()
 
 
 def on_device(ranks, chans, tokens, in_weight, filter_taps, skip_gain, out_weight, grad_out):
@@ -348,6 +449,15 @@
     piece = (ranks, 2 * per, LANES)
     chunk = (chips, block, local_ch)
     wide = (chips, block, feats)
+
+    def travel(count):
+        shapes = (
+            (3, 2, block, count // 2),
+            (2, 2, block // 2, count // 2),
+            (2, 2, block, count // 2),
+        )
+        return [pltpu.VMEM(shape, BF16) for shape in shapes]
+
     scratch = [
         pltpu.VMEM(tokens.shape, BF16),
         pltpu.VMEM(weight.shape, BF16),
@@ -366,19 +476,18 @@
         pltpu.VMEM((block, local_ch), F32),
         pltpu.VMEM((half, 2 * LANES), F32),
         pltpu.VMEM((half, 2 * LANES), F32),
+        pltpu.VMEM((half, 2 * LANES), F32),
         *[pltpu.VMEM(piece, BF16) for _ in range(12)],
         pltpu.VMEM(chunk, BF16),
         pltpu.VMEM(chunk, BF16),
         pltpu.VMEM(chunk, F32),
-        pltpu.VMEM(chunk, BF16),
-        pltpu.VMEM(chunk, BF16),
+        *travel(local_ch),
         pltpu.VMEM((chans, block, local_ch), BF16),
         pltpu.VMEM((3, block, local_ch), BF16),
         pltpu.VMEM(wide, BF16),
         pltpu.VMEM(wide, BF16),
         pltpu.VMEM(wide, F32),
-        pltpu.VMEM(wide, BF16),
-        pltpu.VMEM(wide, BF16),
+        *travel(feats),
         pltpu.VMEM((block, feats), BF16),
         pltpu.VMEM((block, feats), BF16),
         pltpu.VMEM((block, local_ch), F32),
@@ -390,12 +499,14 @@
         pltpu.SemaphoreType.DMA((chips,)),
         pltpu.SemaphoreType.DMA((chips,)),
         pltpu.SemaphoreType.DMA((2,)),
-        pltpu.SemaphoreType.DMA((chips,)),
-        pltpu.SemaphoreType.DMA((chips,)),
+        pltpu.SemaphoreType.DMA((2, 2)),
+        pltpu.SemaphoreType.DMA((2, 2)),
+        pltpu.SemaphoreType.DMA((2, 2, 2)),
+        pltpu.SemaphoreType.DMA((2, 2, 2)),
         pltpu.SemaphoreType.DMA,
         pltpu.SemaphoreType.DMA((chans,)),
     ]
-    return pl.pallas_call(
+    results = pl.pallas_call(
         functools.partial(kernel, ranks, chans),
         out_shape=(
             jax.ShapeDtypeStruct((block, feats), BF16),
@@ -412,6 +523,13 @@
         tokens, weight, filter_taps, skip_gain.reshape(1, local_ch), out_weight, grad_out,
         *[jnp.asarray(table) for table in constants],
     )
+    return pl.pallas_call(
+        place,
+        out_shape=tuple(jax.ShapeDtypeStruct(r.shape, r.dtype) for r in results),
+        in_specs=[vmem] * 3,
+        out_specs=(hbm,) * 3,
+        scratch_shapes=[pltpu.SemaphoreType.DMA((3,))],
+    )(*results)
 
 
 def solution(mesh):

time: 61.5 us -> 54.3 us (0.88)
  local copies, waits for them, and re-layouts: 5.01 us -> 0 us
  Pallas kernels: 55.7 us -> 53 us
    unnamed x3 -> x0, local copies, waits for them, and re-layouts: 5.01 us -> none
    pallas_call x1, Pallas kernels: 55.7 us -> 51 us  [on_device(): pl.pallas_call(functools.partial(kernel, ranks, chans), out_shape=(jax.Sh...]
    pallas_call x0 -> x1, Pallas kernels: none -> 2.01 us  [on_device(): pl.pallas_call(place, out_shape=tuple((jax.ShapeDtypeStruct(r.shape, r.dt...]
where the time goes in v1:
time: 54.3 us; the launch traced here: 53.7 us
  Pallas kernels  53 us (98%)
  between operations  0.64 us (1%)
    pallas_call x1, Pallas kernels, on_device(): pl.pallas_call(functools.partial(kernel, ranks, chans), out_shape=(jax.Sh...  51 us
    pallas_call x1, Pallas kernels, on_device(): pl.pallas_call(place, out_shape=tuple((jax.ShapeDtypeStruct(r.shape, r.dt...  2.01 us

profile of v1, /device:TPU:1, one launch (start us, length us, event | category | flops | bytes accessed | tf_op | source)
XLA Modules:
  0.0 53.7 jit_solution(2253865301071441136)
XLA Ops:
  0.6 51.0 %shard_map.139 = (bf16[256,512]{1,0:T(8,128)(2,1)}, bf16[256,512]{1,0:T(8,128)(2,1)}, f32[256,256]{1,0:T(8,128)}) custom-call(bf16[256,4096]{1,0:T(8,128)(2,1)} %refs_0_.1, bf16[3,4096,256]{2,1,0:T(8,128)(2,1)} %bitcast.2, f32[256,256]{1,0:T(8,128)} %refs_2_.1, f32[1,256]{1,0:T(1,128)} %bitcast.3, bf16[2048,512]{1,0:T(8,128)(2,1)} %refs_4_.1, ...), custom_call_target="tpu_custom_call" | custom-call | tf_op jit(solution)/shard_map/pallas_call | solution.py:509
  51.6 2.0 %shard_map.140 = (bf16[256,512]{1,0:T(8,128)(2,1)}, bf16[256,512]{1,0:T(8,128)(2,1)}, f32[256,256]{1,0:T(8,128)}) custom-call(bf16[256,512]{1,0:T(8,128)(2,1)} %get-tuple-element.6.a, bf16[256,512]{1,0:T(8,128)(2,1)} %get-tuple-element.7.b, f32[256,256]{1,0:T(8,128)} %get-tuple-element.8.c), custom_call_target="tpu_custom_call" | custom-call | tf_op jit(solution)/shard_map/pallas_call | solution.py:526

commit v2 on v1

--- a/solution.py
+++ b/solution.py
@@ -76,7 +76,7 @@
     seq = lax.axis_index("seq")
     ch = lax.axis_index("ch")
     chips = chans // 2
-    x, core = ch // 2, ch % 2
+    x, core = lax.div(ch, 2), lax.rem(ch, 2)
     partner = (seq, ch + 1 - 2 * core)
     block, width = tok.shape
     local_ch = win.shape[2]
@@ -89,15 +89,15 @@
     some = ranks // 2
 
     def peer(step):
-        return (x + step) % chips
+        return lax.rem(x + step, chips)
 
     def slot_of(rank):
-        z, y = rank // turns, rank % turns
-        return (z % 2) * some + (z // 2) * turns + y
+        z, y = lax.div(rank, turns), lax.rem(rank, turns)
+        return lax.rem(z, 2) * some + lax.div(z, 2) * turns + y
 
     def rank_of(slot):
-        side, rest = slot // some, slot % some
-        return (2 * (rest // turns) + side) * turns + rest % turns
+        side, rest = lax.div(slot, some), lax.rem(slot, some)
+        return (2 * lax.div(rest, turns) + side) * turns + lax.rem(rest, turns)
 
     mine = slot_of(seq)
 
@@ -118,7 +118,7 @@
 
     def greet(k, carry):
         pl.semaphore_signal(
-            barrier, inc=1, device_id=((seq + k) % ranks, ch), device_id_type=MESH
+            barrier, inc=1, device_id=(lax.rem(seq + k, ranks), ch), device_id_type=MESH
         )
         return carry
 
@@ -139,20 +139,25 @@
     def wait(ref, sem):
         pltpu.make_async_copy(ref, ref, sem).wait()
 
+    def rounds(send):
+        first = ranks * 3 // 8
+        lax.fori_loop(max(first, 1), ranks, send, 0, unroll=True)
+        lax.fori_loop(1, first, send, 0, unroll=True)
+
     def spread(buf, got, n):
         def send(k, carry):
-            to = (seq + k) % ranks
+            to = lax.rem(seq + k, ranks)
             remote(
                 buf.at[slot_of(to)], got.at[seq], seq_send.at[n], seq_recv.at[n], (to, ch)
             )
             return carry
 
-        lax.fori_loop(1, ranks, send, 0)
+        rounds(send)
         got[seq] = buf[mine]
 
     def spread_side(buf, got, n, side):
         def send(k, carry):
-            slot = side * some + (mine + k) % some
+            slot = side * some + lax.rem(mine + k, some)
             to = rank_of(slot)
 
             @pl.when(to != seq)
@@ -163,15 +168,15 @@
 
             return carry
 
-        lax.fori_loop(0, some, send, 0)
+        lax.fori_loop(0, some, send, 0, unroll=True)
 
     def give_back(buf, got, n):
         def send(k, carry):
-            to = (seq + k) % ranks
+            to = lax.rem(seq + k, ranks)
             remote(buf.at[to], got.at[mine], seq_send.at[n], seq_recv.at[n], (to, ch))
             return carry
 
-        lax.fori_loop(1, ranks, send, 0)
+        rounds(send)
         got[mine] = buf[seq]
 
     def arrive(got, n):
@@ -270,49 +275,47 @@
             into[0, h].astype(F32) + into[1, h].astype(F32)
         )
 
-    copies[0].wait()
-    to_pieces(taps[...] * scale, s_taps, 0)
-    pl.semaphore_wait(barrier, ranks - 1 + 1 + 3)
-    spread(s_taps, r_taps, 0)
-
-    copies[1].wait()
-    copies[2].wait()
-    for copy in copies[3:7]:
-        copy.start()
-
     def feature_chunk(index):
         weights = wout[pl.ds(pl.multiple_of(index * local_ch, local_ch), local_ch), :]
         return dot_nt(gout[...], weights)
 
+    copies[0].wait()
+    for copy in copies[3:]:
+        copy.start()
+    to_pieces(taps[...] * scale, s_taps, 0)
+    copies[1].wait()
+    copies[2].wait()
     for k in (2, 1, 3, 0):
         to = peer(k)
         a_send[to] = feature_chunk(2 * to + 1 - core).astype(BF16)
+    pl.semaphore_wait(barrier, ranks - 1 + 1 + 3)
+    for k in (2, 1, 3, 0):
+        to = peer(k)
         remote(a_send.at[to], a_got.at[to], pair_send.at[0], a_sem.at[to], partner)
+    spread(s_taps, r_taps, 0)
     for k in (2, 1, 3, 0):
         to = peer(k)
         a_own[to] = feature_chunk(2 * to + core)
     fold(a_own, a_got, a_sem, 2)
     far(a_own, a_sum, a_fwd, a_f_sem, 0, 0)
+    far(a_own, a_sum, a_fwd, a_f_sem, 0, 1)
+
+    copies[3].wait()
+    copies[4].wait()
+    mixed[0] = dot(tok[...], win[0]).astype(BF16)
     fold(a_own, a_got, a_sem, 1)
     fold(a_own, a_got, a_sem, 3)
     plain(a_own, a_sum, a_in, a_i_sem, 0, 0)
-    far(a_own, a_sum, a_fwd, a_f_sem, 0, 1)
-    fold(a_own, a_got, a_sem, 0)
-
-    copies[3].wait()
-    copies[4].wait()
-    mixed[0] = dot(tok[...], win[0]).astype(BF16)
-    onward(a_own, a_sum, a_fwd, a_f_sem, a_in, a_i_sem, 0, 0)
     plain(a_own, a_sum, a_in, a_i_sem, 0, 1)
     copies[5].wait()
-    copies[6].wait()
-    for copy in copies[7:]:
-        copy.start()
     mixed[1] = dot(tok[...], win[1]).astype(BF16)
-    onward(a_own, a_sum, a_fwd, a_f_sem, a_in, a_i_sem, 0, 1)
     pre[...] = mixed[1].astype(F32) * mixed[0].astype(F32)
     to_pieces(pre[...], s_pre, 0)
     spread(s_pre, r_pre, 1)
+    onward(a_own, a_sum, a_fwd, a_f_sem, a_in, a_i_sem, 0, 0)
+    onward(a_own, a_sum, a_fwd, a_f_sem, a_in, a_i_sem, 0, 1)
+    fold(a_own, a_got, a_sem, 0)
+    copies[6].wait()
     mixed[2] = dot(tok[...], win[2]).astype(BF16)
 
     for h in (0, 1):
@@ -364,24 +367,33 @@
         total += dot_nt(gm[1], win[1, span, :])
         return total + dot_nt(gm[2], win[2, span, :])
 
-    for k in (2, 1, 3, 0):
+    def to_partner(k):
         to = peer(k)
         b_send[to] = input_chunk(2 * to + 1 - core).astype(BF16)
         remote(b_send.at[to], b_got.at[to], pair_send.at[1], b_sem.at[to], partner)
-    b_own[peer(2)] = input_chunk(2 * peer(2) + core)
+
+    def to_self(k):
+        b_own[peer(k)] = input_chunk(2 * peer(k) + core)
+
+    to_partner(2)
+    to_self(2)
     fold(b_own, b_got, b_sem, 2)
     for h in (0, 1):
         far(b_own, b_sum, b_fwd, b_f_sem, 1, h)
-    for k in (1, 3):
-        b_own[peer(k)] = input_chunk(2 * peer(k) + core)
-        fold(b_own, b_got, b_sem, k)
+    to_partner(1)
+    to_partner(3)
+    give_back(s_gtaps, r_gtaps, 5)
+    to_self(1)
+    to_self(3)
+    fold(b_own, b_got, b_sem, 1)
+    fold(b_own, b_got, b_sem, 3)
     for h in (0, 1):
         plain(b_own, b_sum, b_in, b_i_sem, 1, h)
-    give_back(s_gtaps, r_gtaps, 5)
-    b_own[x] = input_chunk(2 * x + core)
-    fold(b_own, b_got, b_sem, 0)
+    to_partner(0)
     for h in (0, 1):
         onward(b_own, b_sum, b_fwd, b_f_sem, b_in, b_i_sem, 1, h)
+    to_self(0)
+    fold(b_own, b_got, b_sem, 0)
 
     for k in (1, 3, 2):
         slot = 2 * peer(k) + core

time: 54.3 us -> 52.1 us (0.959)
  Pallas kernels: 53 us -> 51.3 us
    pallas_call x1, Pallas kernels: 51 us -> 49.3 us  [on_device(): pl.pallas_call(functools.partial(kernel, ranks, chans), out_shape=(jax.Sh...]
where the time goes in v2:
time: 52.1 us; the launch traced here: 52 us
  Pallas kernels  51.3 us (98%)
  between operations  0.64 us (1%)
    pallas_call x1, Pallas kernels, on_device(): pl.pallas_call(functools.partial(kernel, ranks, chans), out_shape=(jax.Sh...  49.3 us
    pallas_call x1, Pallas kernels, on_device(): pl.pallas_call(place, out_shape=tuple((jax.ShapeDtypeStruct(r.shape, r.dt...  2.01 us

profile of v2, /device:TPU:1, one launch (start us, length us, event | category | flops | bytes accessed | tf_op | source)
XLA Modules:
  0.0 52.0 jit_solution(7138112237673100550)
XLA Ops:
  0.6 49.3 %shard_map.139 = (bf16[256,512]{1,0:T(8,128)(2,1)}, bf16[256,512]{1,0:T(8,128)(2,1)}, f32[256,256]{1,0:T(8,128)}) custom-call(bf16[256,4096]{1,0:T(8,128)(2,1)} %refs_0_.1, bf16[3,4096,256]{2,1,0:T(8,128)(2,1)} %bitcast.2, f32[256,256]{1,0:T(8,128)} %refs_2_.1, f32[1,256]{1,0:T(1,128)} %bitcast.3, bf16[2048,512]{1,0:T(8,128)(2,1)} %refs_4_.1, ...), custom_call_target="tpu_custom_call" | custom-call | tf_op jit(solution)/shard_map/pallas_call | solution.py:521
  50.0 2.0 %shard_map.140 = (bf16[256,512]{1,0:T(8,128)(2,1)}, bf16[256,512]{1,0:T(8,128)(2,1)}, f32[256,256]{1,0:T(8,128)}) custom-call(bf16[256,512]{1,0:T(8,128)(2,1)} %get-tuple-element.6.a, bf16[256,512]{1,0:T(8,128)(2,1)} %get-tuple-element.7.b, f32[256,256]{1,0:T(8,128)} %get-tuple-element.8.c), custom_call_target="tpu_custom_call" | custom-call | tf_op jit(solution)/shard_map/pallas_call | solution.py:538

commit v3 on v2

--- a/solution.py
+++ b/solution.py
@@ -62,7 +62,7 @@
         cross_h, back_h, local_h, unlocal_h, tr_h, ti_h,
         out_h, gtok_h, gtaps_h,
         tok, win, taps, wout, gout, cross, back, local, unlocal, tr, ti,
-        mixed, pre, gg, gc, spec_t, spec_p, spec_g,
+        mixed, pre, gg, gc, spec_t, spec_p, spec_g, early,
         s_taps, s_pre, s_grad, s_conv, s_gpre, s_gtaps,
         r_taps, r_pre, r_grad, r_conv, r_gpre, r_gtaps,
         a_send, a_got, a_own, a_sum, a_fwd, a_in,
@@ -101,6 +101,26 @@
 
     mine = slot_of(seq)
 
+    def rounds(send):
+        first = ranks * 3 // 8
+        lax.fori_loop(max(first, 1), ranks, send, 0, unroll=True)
+        lax.fori_loop(1, first, send, 0, unroll=True)
+
+    barrier = pltpu.get_barrier_semaphore()
+
+    def greet(k, carry):
+        pl.semaphore_signal(
+            barrier, inc=1, device_id=(lax.rem(seq + k, ranks), ch), device_id_type=MESH
+        )
+        return carry
+
+    rounds(greet)
+    pl.semaphore_signal(barrier, inc=1, device_id=partner, device_id_type=MESH)
+    for k in (1, 2, 3):
+        pl.semaphore_signal(
+            barrier, inc=1, device_id=(seq, 2 * peer(k) + core), device_id_type=MESH
+        )
+
     loads = [
         (taps_h, taps), (gout_h, gout), (wout_h, wout), (tok_h, tok),
         (win_h.at[0], win.at[0]), (win_h.at[1], win.at[1]), (win_h.at[2], win.at[2]),
@@ -114,21 +134,6 @@
     for copy in copies[:3]:
         copy.start()
 
-    barrier = pltpu.get_barrier_semaphore()
-
-    def greet(k, carry):
-        pl.semaphore_signal(
-            barrier, inc=1, device_id=(lax.rem(seq + k, ranks), ch), device_id_type=MESH
-        )
-        return carry
-
-    lax.fori_loop(1, ranks, greet, 0)
-    pl.semaphore_signal(barrier, inc=1, device_id=partner, device_id_type=MESH)
-    for k in (1, 2, 3):
-        pl.semaphore_signal(
-            barrier, inc=1, device_id=(seq, 2 * peer(k) + core), device_id_type=MESH
-        )
-
     def remote(src, dst, send, recv, device):
         copy = pltpu.make_async_remote_copy(
             src_ref=src, dst_ref=dst, send_sem=send, recv_sem=recv,
@@ -138,11 +143,6 @@
 
     def wait(ref, sem):
         pltpu.make_async_copy(ref, ref, sem).wait()
-
-    def rounds(send):
-        first = ranks * 3 // 8
-        lax.fori_loop(max(first, 1), ranks, send, 0, unroll=True)
-        lax.fori_loop(1, first, send, 0, unroll=True)
 
     def spread(buf, got, n):
         def send(k, carry):
@@ -157,7 +157,7 @@
 
     def spread_side(buf, got, n, side):
         def send(k, carry):
-            slot = side * some + lax.rem(mine + k, some)
+            slot = side * some + lax.rem(mine + some * 3 // 8 + k, some)
             to = rank_of(slot)
 
             @pl.when(to != seq)
@@ -355,6 +355,10 @@
         )
     remote(gath.at[ch], gath.at[ch], ag_send, ag_sem.at[ch], partner)
     gm[2] = (gg[...] * conv).astype(BF16)
+    for i in (0, 1):
+        owner = 2 * peer(2) + (core if i else 1 - core)
+        span = pl.ds(pl.multiple_of(owner * feats, feats), feats)
+        early[i] = dot_nt(gm[2], win[2, span, :])
 
     arrive(r_gpre, 4)
     grad_pre = from_pieces(r_gpre) + skip_ref[...] * gc[...]
@@ -375,11 +379,36 @@
     def to_self(k):
         b_own[peer(k)] = input_chunk(2 * peer(k) + core)
 
-    to_partner(2)
-    to_self(2)
-    fold(b_own, b_got, b_sem, 2)
-    for h in (0, 1):
+    def half_chunk(i, h):
+        owner = 2 * peer(2) + (core if i else 1 - core)
+        count = feats // 2
+        span = pl.ds(pl.multiple_of(owner * feats + h * count, count), count)
+        total = early[i, :, columns(early, h)] + dot_nt(gm[0], win[0, span, :])
+        return total + dot_nt(gm[1], win[1, span, :])
+
+    to = peer(2)
+    pair_sem = (b_sem.at[to], b_sem.at[chips])
+
+    def half_to_partner(h):
+        cut = columns(b_send, h)
+        b_send[to, :, cut] = half_chunk(0, h).astype(BF16)
+        remote(
+            b_send.at[to, :, cut], b_got.at[to, :, cut], pair_send.at[1], pair_sem[h],
+            partner,
+        )
+
+    def half_far(h):
+        cut = columns(b_own, h)
+        wait(b_got.at[to, :, cut], pair_sem[h])
+        b_own[to, :, cut] = b_own[to, :, cut] + b_got[to, :, cut].astype(F32)
         far(b_own, b_sum, b_fwd, b_f_sem, 1, h)
+
+    half_to_partner(0)
+    b_own[to, :, columns(b_own, 0)] = half_chunk(1, 0)
+    half_to_partner(1)
+    half_far(0)
+    b_own[to, :, columns(b_own, 1)] = half_chunk(1, 1)
+    half_far(1)
     to_partner(1)
     to_partner(3)
     give_back(s_gtaps, r_gtaps, 5)
@@ -390,10 +419,10 @@
     for h in (0, 1):
         plain(b_own, b_sum, b_in, b_i_sem, 1, h)
     to_partner(0)
-    for h in (0, 1):
-        onward(b_own, b_sum, b_fwd, b_f_sem, b_in, b_i_sem, 1, h)
+    onward(b_own, b_sum, b_fwd, b_f_sem, b_in, b_i_sem, 1, 0)
     to_self(0)
     fold(b_own, b_got, b_sem, 0)
+    onward(b_own, b_sum, b_fwd, b_f_sem, b_in, b_i_sem, 1, 1)
 
     for k in (1, 3, 2):
         slot = 2 * peer(k) + core
@@ -419,10 +448,15 @@
     gtaps_copy = pltpu.make_async_copy(o_gtaps, gtaps_h, store_sem.at[1])
     gtaps_copy.start()
 
+    gtok_copies = []
     for h in (0, 1):
-        o_gtok[:, columns(o_gtok, h)] = collect(b_own, b_in, b_i_sem, h).astype(BF16)
-    gtok_copy = pltpu.make_async_copy(o_gtok, gtok_h, store_sem.at[2])
-    gtok_copy.start()
+        cut = columns(o_gtok, h)
+        o_gtok[:, cut] = collect(b_own, b_in, b_i_sem, h).astype(BF16)
+        copy = pltpu.make_async_copy(
+            o_gtok.at[:, cut], gtok_h.at[:, cut], store_sem.at[2 + h]
+        )
+        copy.start()
+        gtok_copies.append(copy)
 
     for n, buf in enumerate((s_taps, s_pre, s_grad, s_conv, s_gpre, s_gtaps)):
         wait(buf.at[pl.ds(0, ranks - 1)], seq_send.at[n])
@@ -433,18 +467,29 @@
     wait(gath.at[pl.ds(0, 7)], ag_send)
     out_copy.wait()
     gtaps_copy.wait()
-    gtok_copy.wait()
-
-
-def place(a, b, c, d, e, f, sem):
-    copies = [
-        pltpu.make_async_copy(src, dst, sem.at[i])
-        for i, (src, dst) in enumerate(((a, d), (b, e), (c, f)))
-    ]
-    for copy in copies:
-        copy.start()
-    for copy in copies:
+    for copy in gtok_copies:
         copy.wait()
+
+
+def place(a, b, c, d, e, f, va, vb, vc, load_sem, store_sem):
+    loads, stores = [], []
+    for i, (src, held, dst) in enumerate(((a, va, d), (b, vb, e), (c, vc, f))):
+        count = src.shape[0] // 4
+        for j in range(4):
+            cut = pl.ds(j * count, count)
+            loads.append(
+                pltpu.make_async_copy(src.at[cut], held.at[cut], load_sem.at[i, j])
+            )
+            stores.append(
+                pltpu.make_async_copy(held.at[cut], dst.at[cut], store_sem.at[i, j])
+            )
+    for load in loads:
+        load.start()
+    for load, store in zip(loads, stores):
+        load.wait()
+        store.start()
+    for store in stores:
+        store.wait()
 
 
 def on_device(ranks, chans, tokens, in_weight, filter_taps, skip_gain, out_weight, grad_out):
@@ -489,6 +534,7 @@
         pltpu.VMEM((half, 2 * LANES), F32),
         pltpu.VMEM((half, 2 * LANES), F32),
         pltpu.VMEM((half, 2 * LANES), F32),
+        pltpu.VMEM((2, block, feats), F32),
         *[pltpu.VMEM(piece, BF16) for _ in range(12)],
         pltpu.VMEM(chunk, BF16),
         pltpu.VMEM(chunk, BF16),
@@ -504,12 +550,12 @@
         pltpu.VMEM((block, feats), BF16),
         pltpu.VMEM((block, local_ch), F32),
         pltpu.SemaphoreType.DMA((13,)),
-        pltpu.SemaphoreType.DMA((3,)),
+        pltpu.SemaphoreType.DMA((4,)),
         pltpu.SemaphoreType.DMA((6,)),
         pltpu.SemaphoreType.DMA((6,)),
         pltpu.SemaphoreType.DMA((2,)),
         pltpu.SemaphoreType.DMA((chips,)),
-        pltpu.SemaphoreType.DMA((chips,)),
+        pltpu.SemaphoreType.DMA((chips + 1,)),
         pltpu.SemaphoreType.DMA((2,)),
         pltpu.SemaphoreType.DMA((2, 2)),
         pltpu.SemaphoreType.DMA((2, 2)),
@@ -538,9 +584,11 @@
     return pl.pallas_call(
         place,
         out_shape=tuple(jax.ShapeDtypeStruct(r.shape, r.dtype) for r in results),
-        in_specs=[vmem] * 3,
+        in_specs=[hbm] * 3,
         out_specs=(hbm,) * 3,
-        scratch_shapes=[pltpu.SemaphoreType.DMA((3,))],
+        scratch_shapes=[pltpu.VMEM(r.shape, r.dtype) for r in results]
+        + [pltpu.SemaphoreType.DMA((3, 4))] * 2,
+        compiler_params=pltpu.CompilerParams(vmem_limit_bytes=58 * 1024 * 1024),
     )(*results)
 
 

time: 52.1 us -> 51.4 us (0.987)
  Pallas kernels: 51.3 us -> 50.6 us
    pallas_call x1, Pallas kernels: 49.3 us -> 48.6 us  [on_device(): pl.pallas_call(functools.partial(kernel, ranks, chans), out_shape=(jax.Sh...]
where the time goes in v3:
time: 51.4 us; the launch traced here: 51.2 us
  Pallas kernels  50.6 us (98%)
  between operations  0.64 us (1%)
    pallas_call x1, Pallas kernels, on_device(): pl.pallas_call(functools.partial(kernel, ranks, chans), out_shape=(jax.Sh...  48.6 us
    pallas_call x1, Pallas kernels, on_device(): pl.pallas_call(place, out_shape=tuple((jax.ShapeDtypeStruct(r.shape, r.dt...  2 us

profile of v3, /device:TPU:1, one launch (start us, length us, event | category | flops | bytes accessed | tf_op | source)
XLA Modules:
  0.0 51.2 jit_solution(14859715929095617464)
XLA Ops:
  0.6 48.6 %shard_map.139 = (bf16[256,512]{1,0:T(8,128)(2,1)}, bf16[256,512]{1,0:T(8,128)(2,1)}, f32[256,256]{1,0:T(8,128)}) custom-call(bf16[256,4096]{1,0:T(8,128)(2,1)} %refs_0_.1, bf16[3,4096,256]{2,1,0:T(8,128)(2,1)} %bitcast.2, f32[256,256]{1,0:T(8,128)} %refs_2_.1, f32[1,256]{1,0:T(1,128)} %bitcast.3, bf16[2048,512]{1,0:T(8,128)(2,1)} %refs_4_.1, ...), custom_call_target="tpu_custom_call" | custom-call | tf_op jit(solution)/shard_map/pallas_call | solution.py:567
  49.2 2.0 %shard_map.140 = (bf16[256,512]{1,0:T(8,128)(2,1)}, bf16[256,512]{1,0:T(8,128)(2,1)}, f32[256,256]{1,0:T(8,128)}) custom-call(bf16[256,512]{1,0:T(8,128)(2,1)} %get-tuple-element.6.a, bf16[256,512]{1,0:T(8,128)(2,1)} %get-tuple-element.7.b, f32[256,256]{1,0:T(8,128)} %get-tuple-element.8.c), custom_call_target="tpu_custom_call" | custom-call | tf_op jit(solution)/shard_map/pallas_call | solution.py:584

commit v4 on v3

--- a/solution.py
+++ b/solution.py
@@ -282,16 +282,25 @@
     copies[0].wait()
     for copy in copies[3:]:
         copy.start()
-    to_pieces(taps[...] * scale, s_taps, 0)
     copies[1].wait()
     copies[2].wait()
-    for k in (2, 1, 3, 0):
+
+    def a_chunk(k):
         to = peer(k)
         a_send[to] = feature_chunk(2 * to + 1 - core).astype(BF16)
-    pl.semaphore_wait(barrier, ranks - 1 + 1 + 3)
-    for k in (2, 1, 3, 0):
+
+    def a_leave(k):
         to = peer(k)
         remote(a_send.at[to], a_got.at[to], pair_send.at[0], a_sem.at[to], partner)
+
+    a_chunk(2)
+    pl.semaphore_wait(barrier, ranks - 1 + 1 + 3)
+    a_leave(2)
+    for k in (1, 3, 0):
+        a_chunk(k)
+    for k in (1, 3, 0):
+        a_leave(k)
+    to_pieces(taps[...] * scale, s_taps, 0)
     spread(s_taps, r_taps, 0)
     for k in (2, 1, 3, 0):
         to = peer(k)

time: 51.4 us -> 51.5 us (level)
  no operation moved by 1% of the time
where the time goes in v4:
time: 51.5 us; the launch traced here: 51.3 us
  Pallas kernels  50.7 us (98%)
  between operations  0.64 us (1%)
    pallas_call x1, Pallas kernels, on_device(): pl.pallas_call(functools.partial(kernel, ranks, chans), out_shape=(jax.Sh...  48.7 us
    pallas_call x1, Pallas kernels, on_device(): pl.pallas_call(place, out_shape=tuple((jax.ShapeDtypeStruct(r.shape, r.dt...  2 us

profile of v4, /device:TPU:1, one launch (start us, length us, event | category | flops | bytes accessed | tf_op | source)
XLA Modules:
  0.0 51.3 jit_solution(8399200437594530698)
XLA Ops:
  0.6 48.7 %shard_map.139 = (bf16[256,512]{1,0:T(8,128)(2,1)}, bf16[256,512]{1,0:T(8,128)(2,1)}, f32[256,256]{1,0:T(8,128)}) custom-call(bf16[256,4096]{1,0:T(8,128)(2,1)} %refs_0_.1, bf16[3,4096,256]{2,1,0:T(8,128)(2,1)} %bitcast.2, f32[256,256]{1,0:T(8,128)} %refs_2_.1, f32[1,256]{1,0:T(1,128)} %bitcast.3, bf16[2048,512]{1,0:T(8,128)(2,1)} %refs_4_.1, ...), custom_call_target="tpu_custom_call" | custom-call | tf_op jit(solution)/shard_map/pallas_call | solution.py:576
  49.3 2.0 %shard_map.140 = (bf16[256,512]{1,0:T(8,128)(2,1)}, bf16[256,512]{1,0:T(8,128)(2,1)}, f32[256,256]{1,0:T(8,128)}) custom-call(bf16[256,512]{1,0:T(8,128)(2,1)} %get-tuple-element.6.a, bf16[256,512]{1,0:T(8,128)(2,1)} %get-tuple-element.7.b, f32[256,256]{1,0:T(8,128)} %get-tuple-element.8.c), custom_call_target="tpu_custom_call" | custom-call | tf_op jit(solution)/shard_map/pallas_call | solution.py:593
